TPU v7x, 128 devices: a whole 4x4x4 slice. The times are simulated.
128 devices in a mesh: ty: 8 (over x_hi, y), tx: 16 (over z, x_lo, core).
Axes of the slice: x: 4 (x_hi: 2, x_lo: 2; x = x_hi * 2 + x_lo), y: 4, z: 4, core: 2. Of those that a mesh axis runs over, the one named last changes fastest.
Arguments:
- region_state: bfloat16 [8, 16, 256, 1024], P('ty', 'tx'), may hold values from -6 to 6
- global_latent: bfloat16 [65536, 1024], P(('ty', 'tx')), may hold values from -6 to 6
- send_rows: int32 [128, 1024], P(('ty', 'tx')), may hold values from 0 to 511, as said below
- recv_slots: int32 [8, 16, 1024], P('ty', 'tx'), may hold values from 0 to 1023, as said below
- regrid_weight: float32 [8, 16, 256, 4], P('ty', 'tx'), may hold values from 0.2 to 1
- window_mask: int32 [8, 16, 5], P('ty', 'tx'), may hold values from 0 to 1, as said below
- norm_gain: bfloat16 [1024], replicated, may hold values from 0.25 to 1.75
- w_query: bfloat16 [1024, 1024], replicated, may hold values from -0.1875 to 0.1875
- w_key: bfloat16 [1024, 1024], replicated, may hold values from -0.1875 to 0.1875
- w_value: bfloat16 [1024, 1024], replicated, may hold values from -0.1875 to 0.1875
- w_out: bfloat16 [1024, 1024], replicated, may hold values from -0.1875 to 0.1875
- out_grad: bfloat16 [8, 16, 256, 1024], P('ty', 'tx'), may hold values from -6 to 6
Outputs:
- updated: bfloat16 [8, 16, 256, 1024], P('ty', 'tx')
- state_grad: bfloat16 [8, 16, 256, 1024], P('ty', 'tx')
- global_grad: bfloat16 [65536, 1024], P(('ty', 'tx'))
- weight_grads: float32 [4, 1024, 1024], P(None, ('ty', 'tx'))
Inputs may be any that keep to these rules, and one draw needn't show every extreme that they name: `send_rows`: each device's list names each of its 512 global rows equally often. `recv_slots`: on every tile each of the 1024 received slots is read, all about equally often. `window_mask`: entry 0 is 1; a flag is 0 where the tile named lies outside the grid; two neighbouring tiles flag each other alike.
All inputs are finite; a program needn't handle non-finite values.
Results may differ from a plain program's by a relative error of at most 0.015.
Values may be sent and summed in bfloat16 or wider, within the bound.
No kernel may reach another device: no remote copies, remote signals or barrier semaphores. Data moves between devices by JAX's collectives and lax.ppermute only.
A program may use at most 128 MiB of HBM per device.

v0:
```python
import jax
import jax.numpy as jnp
from jax import lax
from jax.sharding import PartitionSpec as P

HEADS = 8
HEAD_SIZE = 128


EPSILON = 1e-05


def padded_2(cells, sides, width):
    for axis, dim in sides:
        count = lax.axis_size(axis)
        ends = count - 1
        head = lax.slice_in_dim(cells, 0, width, axis=dim)
        tail = lax.slice_in_dim(cells, cells.shape[dim] - width, cells.shape[dim], axis=dim)
        cells = jnp.concatenate(
            [
                lax.ppermute(tail, axis, [(i, (i + 1) % count) for i in range(ends)]),
                cells,
                lax.ppermute(head, axis, [((i + 1) % count, i) for i in range(ends)]),
            ],
            axis=dim,
        )
    return cells


def passed_along(block, axis, distance):
    devices = range(lax.axis_size(axis))
    route = [(i - distance, i) for i in devices if i - distance in devices]
    return lax.ppermute(block, axis, route)


def deliver(buffer):
    return lax.all_to_all(buffer, ("ty", "tx"), split_axis=0, concat_axis=0, tiled=True)


def five_pieces(padded):
    return jnp.stack([padded[1, 1], padded[0, 1], padded[2, 1], padded[1, 0], padded[1, 2]])


def head_major(rows):
    return jnp.transpose(rows.reshape(rows.shape[0], HEADS, HEAD_SIZE), (1, 0, 2))


def row_major(heads):
    return jnp.transpose(heads, (1, 0, 2)).reshape(heads.shape[1], HEADS * HEAD_SIZE)


def body(
    region_state,
    global_latent,
    send_rows,
    recv_slots,
    regrid_weight,
    window_mask,
    norm_gain,
    w_query,
    w_key,
    w_value,
    w_out,
    out_grad,
):
    num_rows = region_state.shape[2]
    model_width = region_state.shape[3]
    sources_per = regrid_weight.shape[3]
    attn_scale = HEAD_SIZE ** (-0.5)
    local_state = region_state[0, 0]
    outgoing = global_latent[send_rows[0]]
    incoming = deliver(outgoing)
    slot_ids = recv_slots[0, 0]
    pulled = incoming[slot_ids].reshape(num_rows, sources_per, model_width)
    blend = regrid_weight[0, 0]
    forcing = jnp.sum(blend[:, :, None] * pulled.astype(jnp.float32), axis=1)
    pre_norm = local_state.astype(jnp.float32) + forcing
    inverse = lax.rsqrt(jnp.mean(pre_norm * pre_norm, axis=-1, keepdims=True) + EPSILON)
    normed = pre_norm * inverse
    normed_in = (normed * norm_gain.astype(jnp.float32)).astype(jnp.bfloat16)
    queries = jnp.dot(normed_in, w_query, preferred_element_type=jnp.float32).astype(jnp.bfloat16)
    key_rows = jnp.dot(normed_in, w_key, preferred_element_type=jnp.float32).astype(jnp.bfloat16)
    value_rows = jnp.dot(normed_in, w_value, preferred_element_type=jnp.float32).astype(
        jnp.bfloat16
    )
    paired = jnp.concatenate([key_rows, value_rows], axis=-1)[None, None]
    near = five_pieces(padded_2(paired, (("ty", 0), ("tx", 1)), 1))
    near_keys = head_major(near[..., :model_width].reshape(5 * num_rows, model_width))
    near_values = head_major(near[..., model_width:].reshape(5 * num_rows, model_width))
    valid = jnp.repeat(window_mask[0, 0] > 0, num_rows)
    grad_out = out_grad[0, 0]
    grad_attended = jnp.dot(grad_out, w_out.T, preferred_element_type=jnp.float32).astype(
        jnp.bfloat16
    )

    def one_head(items):
        query_h, key_h, value_h, grad_h = items
        raw = jnp.dot(query_h, key_h.T, preferred_element_type=jnp.float32)
        scores = jnp.where(valid[None, :], raw * attn_scale, -jnp.inf)
        highest = jnp.max(scores, axis=-1, keepdims=True)
        log_total = highest + jnp.log(jnp.sum(jnp.exp(scores - highest), axis=-1, keepdims=True))
        prob_exact = jnp.exp(scores - log_total)
        prob_weights = prob_exact.astype(jnp.bfloat16)
        attended_h = jnp.dot(prob_weights, value_h, preferred_element_type=jnp.float32).astype(
            jnp.bfloat16
        )
        row_delta = jnp.sum(grad_h.astype(jnp.float32) * attended_h.astype(jnp.float32), axis=-1)
        grad_prob = jnp.dot(grad_h, value_h.T, preferred_element_type=jnp.float32)
        dscore = (prob_exact * (grad_prob - row_delta[:, None]) * attn_scale).astype(jnp.bfloat16)
        grad_query_h = jnp.dot(dscore, key_h, preferred_element_type=jnp.float32).astype(
            jnp.bfloat16
        )
        key_part = jnp.dot(dscore.T, query_h, preferred_element_type=jnp.float32)
        value_part = jnp.dot(prob_weights.T, grad_h, preferred_element_type=jnp.float32)
        return (attended_h, grad_query_h, log_total[:, 0], row_delta, key_part, value_part)

    results = lax.map(
        one_head, (head_major(queries), near_keys, near_values, head_major(grad_attended))
    )
    attended = row_major(results[0])
    grad_query = row_major(results[1])
    log_total = results[2]
    row_delta = results[3]
    output_term = jnp.dot(attended, w_out, preferred_element_type=jnp.float32)
    updated = (local_state.astype(jnp.float32) + output_term).astype(jnp.bfloat16)
    key_parts = row_major(results[4]).reshape(5, num_rows, model_width)
    value_parts = row_major(results[5]).reshape(5, num_rows, model_width)
    pieces = jnp.concatenate([key_parts, value_parts], axis=-1)
    summed = pieces[0]
    for slot_index, shift_by in ((1, -1), (2, 1)):
        summed = summed + passed_along(
            pieces[slot_index].astype(jnp.bfloat16), "ty", shift_by
        ).astype(jnp.float32)
    for slot_index, shift_by in ((3, -1), (4, 1)):
        summed = summed + passed_along(
            pieces[slot_index].astype(jnp.bfloat16), "tx", shift_by
        ).astype(jnp.float32)
    key_sum = summed[:, :model_width]
    value_sum = summed[:, model_width:]
    grad_key = key_sum.astype(jnp.bfloat16)
    grad_value = value_sum.astype(jnp.bfloat16)
    grad_normed_in = jnp.dot(grad_query, w_query.T, preferred_element_type=jnp.float32)
    grad_normed_in = grad_normed_in + jnp.dot(grad_key, w_key.T, preferred_element_type=jnp.float32)
    grad_normed_in = grad_normed_in + jnp.dot(
        grad_value, w_value.T, preferred_element_type=jnp.float32
    )
    partial_grads = jnp.stack(
        [
            jnp.dot(normed_in.T, grad_query, preferred_element_type=jnp.float32),
            jnp.dot(normed_in.T, grad_key, preferred_element_type=jnp.float32),
            jnp.dot(normed_in.T, grad_value, preferred_element_type=jnp.float32),
            jnp.dot(attended.T, grad_out, preferred_element_type=jnp.float32),
        ]
    )
    weight_grads = lax.psum_scatter(partial_grads, ("ty", "tx"), scatter_dimension=1, tiled=True)
    grad_normed = grad_normed_in * norm_gain.astype(jnp.float32)
    grad_pre = inverse * (
        grad_normed - normed * jnp.mean(grad_normed * normed, axis=-1, keepdims=True)
    )
    state_grad = (grad_out.astype(jnp.float32) + grad_pre).astype(jnp.bfloat16)
    use_grad = (blend[:, :, None] * grad_pre[:, None, :]).reshape(-1, model_width)
    slot_grad = (
        jnp.zeros((incoming.shape[0], model_width), jnp.float32)
        .at[slot_ids]
        .add(use_grad)
        .astype(jnp.bfloat16)
    )
    returned = deliver(slot_grad)
    global_grad = (
        jnp.zeros((global_latent.shape[0], model_width), jnp.float32)
        .at[send_rows[0]]
        .add(returned.astype(jnp.float32))
    )
    return (
        updated[None, None],
        state_grad[None, None],
        global_grad.astype(jnp.bfloat16),
        weight_grads,
    )


def solution(mesh):
    return jax.shard_map(
        body,
        mesh=mesh,
        in_specs=(
            P("ty", "tx", None, None),
            P(("ty", "tx"), None),
            P(("ty", "tx"), None),
            P("ty", "tx", None),
            P("ty", "tx", None, None),
            P("ty", "tx", None),
            P(),
            P(),
            P(),
            P(),
            P(),
            P("ty", "tx", None, None),
        ),
        out_specs=(
            P("ty", "tx", None, None),
            P("ty", "tx", None, None),
            P(("ty", "tx"), None),
            P(None, ("ty", "tx"), None),
        ),
        check_vma=False,
    )
```

profile of v0, /device:TPU:0, one launch (start us, length us, event | category | flops | bytes accessed | tf_op | source)
XLA Modules:
  0.0 1092.6 jit_solution(12119435817723051233)
XLA Ops:
  8.6 7.4 gather_fusion
  16.0 11.7 %all-to-all-start = ((bf16[128,8,1024]{2,1,0:T(8,128)(2,1)}), bf16[128,8,1024]{2,1,0:T(8,128)(2,1)}, u32[]{:S(2)}, u32[]{:S(2)}) async-start(bf16[128,8,1024]{2,1,0:T(8,128)(2,1)} %bitcast.223), calls=%async_computation | async-start | bytes 4194304 | tf_op jit(solution)/shard_map/all_to_all | solution.py:37
  28.0 29.7 %all-to-all-done = bf16[128,8,1024]{2,1,0:T(8,128)(2,1)} async-done(((bf16[128,8,1024]{2,1,0:T(8,128)(2,1)}), bf16[128,8,1024]{2,1,0:T(8,128)(2,1)}, u32[]{:S(2)}, u32[]{:S(2)}) %all-to-all-start) | async-done | bytes 2097184 | tf_op jit(solution)/shard_map/all_to_all | solution.py:37
  57.7 7.9 gather_fusion.1
  70.4 4.9 multiply_reduce_fusion.1
  81.1 20.9 %collective-permute-done = bf16[1,1,256,2048]{3,2,1,0:T(8,128)(2,1)S(1)} collective-permute-done((bf16[1,1,256,2048]{3,2,1,0:T(8,128)(2,1)S(1)}, bf16[1,1,256,2048]{3,2,1,0:T(8,128)(2,1)S(1)}, u32[]{:S(2)}, u32[]{:S(2)}) %collective-permute-start) | collective-permute-done | bytes 1048608 | tf_op jit(solution)/shard_map/ppermute | solution.py:21
  130.6 114.2 %while.17 = (s32[]{:T(128)}, bf16[8,256,128]{1,2,0:T(8,128)(2,1)}, bf16[8,256,128]{1,2,0:T(8,128)(2,1)}, f32[8,1280,128]{2,1,0:T(8,128)}, f32[8,1280,128]{2,1,0:...) while((s32[]{:T(128)}, bf16[8,256,128]{1,2,0:T(8,128)(2,1)}, ...), condition=%wide.region_6.7_spmd.clone, body=%wide.region_2.6_spmd.clone.sunk | while | flops 508100096 | bytes 14636194 | solution.py:117
  244.8 9.4 copy.29
  254.2 6.8 reshape_reshape.14
  261.1 5.9 constant_dynamic-update-slice_fusion.2
  266.9 8.3 copy.30
  275.2 6.7 reshape_reshape.15
  281.9 5.7 constant_dynamic-update-slice_fusion.1
  287.6 4.8 convert.13
  293.1 59.6 %collective-permute-start.7 = (bf16[256,2048]{1,0:T(8,128)(2,1)S(1)}, bf16[256,2048]{1,0:T(8,128)(2,1)S(1)}, u32[]{:S(2)}, u32[]{:S(2)}) collective-permute-start(bf16[256,2048]{1,0:T(8,128)(2,1)S(1)} %get-tuple-element.133), channel_id=1, source_target_pairs={{0,1},{1,2},{2,3},{3,4},{4,5},{5,6},{6,7},{7,8},{8,9},{9,10},{10,1... | collective-permute-start | bytes 3145736 | tf_op jit(solution)/shard_map/ppermute | solution.py:33
  360.2 19.4 %collective-permute-done.5 = bf16[256,2048]{1,0:T(8,128)(2,1)S(1)} collective-permute-done((bf16[256,2048]{1,0:T(8,128)(2,1)S(1)}, bf16[256,2048]{1,0:T(8,128)(2,1)S(1)}, u32[]{:S(2)}, u32[]{:S(2)}) %collective-permute-start.5) | collective-permute-done | bytes 1048608 | tf_op jit(solution)/shard_map/ppermute | solution.py:33
  379.6 5.3 collective-permute-done.4
  389.1 6.1 pad_maximum_fusion
  404.7 5.3 mul.108
  410.0 12.8 %scatter_custom_fusion = f32[1024,1024]{1,0:T(8,128)} fusion(s32[1024]{0:T(1024)} %bitcast.238, f32[1024,1024]{1,0:T(8,128)} %mul.108, f32[1024]{0:T(1024)S(1)} %mul.105, f32[]{:T(128)} %constant.11.clone.1), kind=kCustom, calls=%fused_computation.50 | custom fusion | flops 2097152 | bytes 8393216 | tf_op jit(solution)/shard_map/scatter-add | solution.py:165
  426.6 27.8 %all-to-all-start.1 = ((bf16[128,8,1024]{2,1,0:T(8,128)(2,1)}), bf16[128,8,1024]{2,1,0:T(8,128)(2,1)}, u32[]{:S(2)}, u32[]{:S(2)}) async-start(bf16[128,8,1024]{2,1,0:T(8,128)(2,1)} %convert_bitcast_fusion), calls=%async_computation.1 | async-start | bytes 4194304 | tf_op jit(solution)/shard_map/all_to_all | solution.py:37
  457.6 32.8 %all-to-all-done.1 = bf16[128,8,1024]{2,1,0:T(8,128)(2,1)} async-done(((bf16[128,8,1024]{2,1,0:T(8,128)(2,1)}), bf16[128,8,1024]{2,1,0:T(8,128)(2,1)}, u32[]{:S(2)}, u32[]{:S(2)}) %all-to-all-start.1) | async-done | bytes 2097184 | tf_op jit(solution)/shard_map/all_to_all | solution.py:37
  490.3 11.1 %scatter_custom_fusion.1 = f32[512,1024]{1,0:T(8,128)} fusion(s32[1024]{0:T(1024)} %bitcast.236, bf16[128,8,1024]{2,1,0:T(8,128)(2,1)} %all-to-all-done.1, f32[]{:T(128)} %constant.11.clone.1), kind=kCustom, calls=%fused_computation.48 | custom fusion | flops 2097152 | bytes 4194816 | tf_op jit(solution)/shard_map/scatter-add | solution.py:172
  504.2 581.2 %reduce-scatter.2.cloned.1.call-done = f32[4,8,1024]{2,1,0:T(8,128)} async-done(((f32[4,1024,1024]{2,1,0:T(8,128)}), f32[4,8,1024]{2,1,0:T(8,128)}) %reduce-scatter.2.cloned.1.call-update) | async-done | bytes 131088 | tf_op jit(solution)/shard_map/reduce_scatter | solution.py:155
  (254 shorter events, 185.7 us)
Async XLA Ops:
  7.2 68.6 %copy-start = (bf16[1024,1024]{1,0:T(8,128)(2,1)S(1)}, bf16[1024,1024]{1,0:T(8,128)(2,1)}, u32[]{:S(2)}) copy-start(bf16[1024,1024]{1,0:T(8,128)(2,1)} %param.23) | copy-start | bytes 6291460
  16.0 11.8 %copy-start.28 = (f32[1,1,256,4]{2,3,1,0:T(4,128)S(1)}, f32[1,1,256,4]{2,3,1,0:T(4,128)}, u32[]{:S(2)}) copy-start(f32[1,1,256,4]{2,3,1,0:T(4,128)} %param.18) | copy-start | bytes 12292
  16.0 11.9 %copy-start.31 = (s32[1,1,1024]{2,1,0:T(1,128)S(1)}, s32[1,1,1024]{2,1,0:T(1,128)}, u32[]{:S(2)}) copy-start(s32[1,1,1024]{2,1,0:T(1,128)} %param.17) | copy-start | bytes 12292
  16.0 41.7 %all-to-all-start = ((bf16[128,8,1024]{2,1,0:T(8,128)(2,1)}), bf16[128,8,1024]{2,1,0:T(8,128)(2,1)}, u32[]{:S(2)}, u32[]{:S(2)}) async-start(bf16[128,8,1024]{2,1,0:T(8,128)(2,1)} %bitcast.223), calls=%async_computation | async-start | bytes 4194304 | tf_op jit(solution)/shard_map/all_to_all | solution.py:37
  27.7 1057.6 %reduce-scatter.2.cloned.1.call-start = ((), (), s32[]{:S(2)}) async-start(), calls=%async_computation.3 | async-start | bytes 16908288 | tf_op jit(solution)/shard_map/reduce_scatter | solution.py:155
  28.0 37.7 %copy-start.30 = (s32[1024,1]{0,1:T(1,128)}, s32[1024,1]{0,1:T(1,128)S(1)}, u32[]{:S(2)}) copy-start(s32[1024,1]{0,1:T(1,128)S(1)} %compare_select_fusion) | copy-start | bytes 12292
  75.8 42.8 %copy-start.8 = (bf16[256,1024]{1,0:T(8,128)(2,1)}, bf16[256,1024]{1,0:T(8,128)(2,1)S(1)}, u32[]{:S(2)}) copy-start(bf16[256,1024]{1,0:T(8,128)(2,1)S(1)} %multiply_convert_fusion) | copy-start | bytes 1572868
  78.2 30.0 %copy-start.26 = (bf16[256,1024]{1,0:T(8,128)(2,1)}, bf16[256,1024]{1,0:T(8,128)(2,1)S(1)}, u32[]{:S(2)}) copy-start(bf16[256,1024]{1,0:T(8,128)(2,1)S(1)} %convolution_convert_fusion.4) | copy-start | bytes 1572868
  78.3 34.5 %copy-start.21 = (bf16[1,1,256,1024]{3,2,1,0:T(8,128)(2,1)S(1)}, bf16[1,1,256,1024]{3,2,1,0:T(8,128)(2,1)}, u32[]{:S(2)}) copy-start(bf16[1,1,256,1024]{3,2,1,0:T(8,128)(2,1)} %param.25) | copy-start | bytes 1572868
  78.4 23.7 %collective-permute-start = (bf16[1,1,256,2048]{3,2,1,0:T(8,128)(2,1)S(1)}, bf16[1,1,256,2048]{3,2,1,0:T(8,128)(2,1)S(1)}, u32[]{:S(2)}, u32[]{:S(2)}) collective-permute-start(bf16[1,1,256,2048]{3,2,1,0:T(8,128)(2,1)S(1)} %fusion.57), channel_id=1, source_target_pairs={{0,16},{16,32},{32,48},{48,64},{64,80},{80,96},{96,112},{1,17},{17... | collective-permute-start | bytes 3145736 | tf_op jit(solution)/shard_map/ppermute | solution.py:21
  79.8 26.4 %collective-permute-start.1 = (bf16[1,1,256,2048]{3,2,1,0:T(8,128)(2,1)S(1)}, bf16[1,1,256,2048]{3,2,1,0:T(8,128)(2,1)S(1)}, u32[]{:S(2)}, u32[]{:S(2)}) collective-permute-start(bf16[1,1,256,2048]{3,2,1,0:T(8,128)(2,1)S(1)} %fusion.57), channel_id=1, source_target_pairs={{16,0},{32,16},{48,32},{64,48},{80,64},{96,80},{112,96},{17,1},{33... | collective-permute-start | bytes 3145736 | tf_op jit(solution)/shard_map/ppermute | solution.py:23
  108.3 14.2 %collective-permute-start.2 = (bf16[3,1,256,2048]{3,2,1,0:T(8,128)(2,1)}, bf16[3,1,256,2048]{3,2,1,0:T(8,128)(2,1)}, u32[]{:S(2)}, u32[]{:S(2)}) collective-permute-start(bf16[3,1,256,2048]{3,2,1,0:T(8,128)(2,1)} %pad_maximum_fusion.1), channel_id=1, source_target_pairs={{0,1},{1,2},{2,3},{3,4},{4,5},{5,6},{6,7},{7,8},{8,9},{9,10},{10,1... | collective-permute-start | bytes 9437192 | tf_op jit(solution)/shard_map/ppermute | solution.py:21
  111.3 12.5 %collective-permute-start.3 = (bf16[3,1,256,2048]{3,2,1,0:T(8,128)(2,1)}, bf16[3,1,256,2048]{3,2,1,0:T(8,128)(2,1)}, u32[]{:S(2)}, u32[]{:S(2)}) collective-permute-start(bf16[3,1,256,2048]{3,2,1,0:T(8,128)(2,1)} %pad_maximum_fusion.1), channel_id=1, source_target_pairs={{1,0},{2,1},{3,2},{4,3},{5,4},{6,5},{7,6},{8,7},{9,8},{10,9},{11,1... | collective-permute-start | bytes 9437192 | tf_op jit(solution)/shard_map/ppermute | solution.py:23
  254.2 12.7 %slice-start = ((s8[5242880]{0:T(1024)(128)(4,1)}), s8[1048576]{0:T(1024)(128)(4,1)S(1)}, s32[]{:S(2)}) async-start(s8[5242880]{0:T(1024)(128)(4,1)} %bitcast.225), calls=%async_computation.4 | async-start | bytes 2097152
  292.4 65.3 %copy-start.16 = (bf16[8,256,128]{1,2,0:T(8,128)(2,1)S(1)}, bf16[8,256,128]{1,2,0:T(8,128)(2,1)}, u32[]{:S(2)}) copy-start(bf16[8,256,128]{1,2,0:T(8,128)(2,1)} %get-tuple-element.59) | copy-start | bytes 1572868
  292.5 65.3 %copy-start.22 = (bf16[1,1,256,1024]{3,2,1,0:T(8,128)(2,1)S(1)}, bf16[1,1,256,1024]{3,2,1,0:T(8,128)(2,1)}, u32[]{:S(2)}) copy-start(bf16[1,1,256,1024]{3,2,1,0:T(8,128)(2,1)} %param.25) | copy-start | bytes 1572868
  293.1 67.1 %collective-permute-start.7 = (bf16[256,2048]{1,0:T(8,128)(2,1)S(1)}, bf16[256,2048]{1,0:T(8,128)(2,1)S(1)}, u32[]{:S(2)}, u32[]{:S(2)}) collective-permute-start(bf16[256,2048]{1,0:T(8,128)(2,1)S(1)} %get-tuple-element.133), channel_id=1, source_target_pairs={{0,1},{1,2},{2,3},{3,4},{4,5},{5,6},{6,7},{7,8},{8,9},{9,10},{10,1... | collective-permute-start | bytes 3145736 | tf_op jit(solution)/shard_map/ppermute | solution.py:33
  352.7 7.5 collective-permute-start.6
  354.0 25.6 %collective-permute-start.5 = (bf16[256,2048]{1,0:T(8,128)(2,1)S(1)}, bf16[256,2048]{1,0:T(8,128)(2,1)S(1)}, u32[]{:S(2)}, u32[]{:S(2)}) collective-permute-start(bf16[256,2048]{1,0:T(8,128)(2,1)S(1)} %get-tuple-element.135), channel_id=1, source_target_pairs={{0,16},{16,32},{32,48},{48,64},{64,80},{80,96},{96,112},{1,17},{17... | collective-permute-start | bytes 3145736 | tf_op jit(solution)/shard_map/ppermute | solution.py:33
  356.5 28.4 %collective-permute-start.4 = (bf16[256,2048]{1,0:T(8,128)(2,1)S(1)}, bf16[256,2048]{1,0:T(8,128)(2,1)S(1)}, u32[]{:S(2)}, u32[]{:S(2)}) collective-permute-start(bf16[256,2048]{1,0:T(8,128)(2,1)S(1)} %get-tuple-element.132), channel_id=1, source_target_pairs={{16,0},{32,16},{48,32},{64,48},{80,64},{96,80},{112,96},{17,1},{33... | collective-permute-start | bytes 3145736 | tf_op jit(solution)/shard_map/ppermute | solution.py:33
  360.2 27.2 %copy-start.9 = (bf16[256,1024]{1,0:T(8,128)(2,1)S(1)}, bf16[256,1024]{1,0:T(8,128)(2,1)}, u32[]{:S(2)}) copy-start(bf16[256,1024]{1,0:T(8,128)(2,1)} %copy-done.8) | copy-start | bytes 1572868
  426.6 27.8 %copy-start.7 = (bf16[1,1,256,1024]{3,2,1,0:T(8,128)(2,1)S(1)}, bf16[1,1,256,1024]{3,2,1,0:T(8,128)(2,1)}, u32[]{:S(2)}) copy-start(bf16[1,1,256,1024]{3,2,1,0:T(8,128)(2,1)} %param.14) | copy-start | bytes 1572868
  426.6 27.8 %copy-start.17 = (bf16[8,256,128]{1,2,0:T(8,128)(2,1)S(1)}, bf16[8,256,128]{1,2,0:T(8,128)(2,1)}, u32[]{:S(2)}) copy-start(bf16[8,256,128]{1,2,0:T(8,128)(2,1)} %get-tuple-element.59) | copy-start | bytes 1572868
  426.6 63.7 %all-to-all-start.1 = ((bf16[128,8,1024]{2,1,0:T(8,128)(2,1)}), bf16[128,8,1024]{2,1,0:T(8,128)(2,1)}, u32[]{:S(2)}, u32[]{:S(2)}) async-start(bf16[128,8,1024]{2,1,0:T(8,128)(2,1)} %convert_bitcast_fusion), calls=%async_computation.1 | async-start | bytes 4194304 | tf_op jit(solution)/shard_map/all_to_all | solution.py:37
  (30 other events, 79.1 us)
Sparse Core Ops, SparseCore 0:
  395.3 689.9 reduce-scatter.1
where the time goes:
time: 1100 us; the launch traced here: 1090 us
  waiting for transfers between devices  693 us (63%)
  starting transfers between devices  111 us (10%)
  local copies, waits for them, and re-layouts  105 us (10%)
  matrix products  103 us (9%)
  other arithmetic  63.8 us (6%)
  between operations  15.1 us (1%)
    reduce_scatter x1, waiting for transfers between devices, body(): lax.psum_scatter(partial_grads, ('ty', 'tx'), scatter_dimension=1, tiled=...  581 us
    ppermute x4, starting transfers between devices, passed_along(): return lax.ppermute(block, axis, route)  64.7 us
    all_to_all x2, waiting for transfers between devices, deliver(): lax.all_to_all(buffer, ('ty', 'tx'), split_axis=0, concat_axis=0, tiled=T...  62.5 us
    all_to_all x2, starting transfers between devices, deliver(): lax.all_to_all(buffer, ('ty', 'tx'), split_axis=0, concat_axis=0, tiled=T...  39.5 us
    ppermute x4, waiting for transfers between devices, passed_along(): return lax.ppermute(block, axis, route)  24.7 us
  transfers between devices with their start and end apart: 11, of which 7 were waited for; matrix products, arithmetic and copies ran while one was open for 6% of the time, Pallas kernels for 0%

commit v1 on v0

v1 whole, which is shorter than its diff:
```python
import functools
import jax
import jax.numpy as jnp
from jax import lax
from jax.experimental import pallas as pl
from jax.experimental.pallas import tpu as pltpu
from jax.sharding import PartitionSpec as P

HEADS = 8
HEAD_SIZE = 128
EPSILON = 1e-05
LOG2_E = 1.4426950408889634
BF16 = jnp.bfloat16
F32 = jnp.float32
NN = (((1,), (0,)), ((), ()))
NT = (((1,), (1,)), ((), ()))
TN = (((0,), (0,)), ((), ()))


def mm(left, right, dims=NN):
    return lax.dot_general(left, right, dims, preferred_element_type=F32)


def params(**more):
    return pltpu.CompilerParams(vmem_limit_bytes=56 * 1024 * 1024, **more)


def pick_kernel(rows_ref, table_ref, out_ref):
    table_rows = table_ref.shape[0]
    hit = lax.broadcasted_iota(jnp.int32, (table_rows, rows_ref.shape[1]), 0) == rows_ref[...]
    out_ref[...] = mm(hit.astype(F32).astype(BF16), table_ref[...], TN).astype(BF16)


def pick_rows(rows, table):
    count, width, step = rows.shape[1], table.shape[1], 256
    return pl.pallas_call(
        pick_kernel,
        grid=(count // step,),
        in_specs=[
            pl.BlockSpec((1, step), lambda i: (0, i)),
            pl.BlockSpec(table.shape, lambda i: (0, 0)),
        ],
        out_specs=pl.BlockSpec((step, width), lambda i: (i, 0)),
        out_shape=jax.ShapeDtypeStruct((count, width), BF16),
        compiler_params=params(),
        name="pick_rows",
    )(rows, table)


def add_kernel(rows_ref, sent_ref, out_ref):
    step = out_ref.shape[0]
    ids = lax.broadcasted_iota(jnp.int32, (step, rows_ref.shape[1]), 0) + pl.program_id(0) * step
    hit = (ids == rows_ref[...]).astype(F32).astype(BF16)
    out_ref[...] = mm(hit, sent_ref[...]).astype(BF16)


def add_rows(rows, sent, table_rows):
    step = 256
    return pl.pallas_call(
        add_kernel,
        grid=(table_rows // step,),
        in_specs=[
            pl.BlockSpec(rows.shape, lambda i: (0, 0)),
            pl.BlockSpec(sent.shape, lambda i: (0, 0)),
        ],
        out_specs=pl.BlockSpec((step, sent.shape[1]), lambda i: (i, 0)),
        out_shape=jax.ShapeDtypeStruct((table_rows, sent.shape[1]), BF16),
        compiler_params=params(),
        name="add_rows",
    )(rows, sent)


def blend_kernel(slots_ref, blend_ref, incoming_ref, state_ref, gain_ref, in_ref, normed_ref, inverse_ref, high_ref, low_ref):
    rows, slots = blend_ref.shape[0], incoming_ref.shape[0]
    lanes = lax.broadcasted_iota(jnp.int32, (rows, slots), 1)
    spread = jnp.zeros((rows, slots), F32)
    for k in range(blend_ref.shape[1]):
        spread = spread + jnp.where(lanes == slots_ref[:, k : k + 1], blend_ref[:, k : k + 1], 0.0)
    high = spread.astype(BF16)
    low = (spread - high.astype(F32)).astype(BF16)
    high_ref[...] = high
    low_ref[...] = low
    incoming = incoming_ref[...]
    pre = state_ref[...].astype(F32) + (mm(high, incoming) + mm(low, incoming))
    inverse = lax.rsqrt(jnp.mean(pre * pre, axis=-1, keepdims=True) + EPSILON)
    normed = pre * inverse
    normed_ref[...] = normed
    inverse_ref[...] = jnp.broadcast_to(inverse, inverse_ref.shape)
    in_ref[...] = (normed * gain_ref[...].astype(F32)).astype(BF16)


def blend_norm(slots, blend, incoming, state, gain):
    rows, width = state.shape
    spread = jax.ShapeDtypeStruct((rows, incoming.shape[0]), BF16)
    return pl.pallas_call(
        blend_kernel,
        out_shape=(
            jax.ShapeDtypeStruct((rows, width), BF16),
            jax.ShapeDtypeStruct((rows, width), F32),
            jax.ShapeDtypeStruct((rows, 128), F32),
            spread,
            spread,
        ),
        compiler_params=params(),
        name="blend_norm",
    )(slots, blend, incoming, state, gain)


def attend_kernel(
    chunk, mask_ref, own_ref, up_ref, down_ref, left_ref, right_ref, state_ref, grad_ref, wq_ref, wk_ref, wv_ref, wo_ref,
    updated_ref, own_grad_ref, near_grad_ref, qkv_ref, out_ref,
    x_all, x_turned, grads, total,
):
    head = pl.program_id(0)
    rows = own_ref.shape[0]
    blocks = x_all.shape[0] // rows

    @pl.when(head == 0)
    def _():
        for b, ref in enumerate((own_ref, up_ref, down_ref, left_ref, right_ref)):
            x_all[b * rows : (b + 1) * rows] = ref[...]
            x_turned[:, b * rows : (b + 1) * rows] = ref[...].T
        grads[...] = jnp.zeros_like(grads)
        total[...] = jnp.zeros_like(total)

    w_both = jnp.concatenate([wk_ref[...], wv_ref[...]], axis=1)
    grad_out = grad_ref[...]
    query_t = mm(wq_ref[...], own_ref[...], (((0,), (1,)), ((), ()))).astype(BF16)
    query = query_t.astype(F32).T.astype(BF16)
    g_t = mm(wo_ref[...], grad_out, NT).astype(BF16)
    g = g_t.astype(F32).T.astype(BF16)
    both = mm(x_all[...], w_both).astype(BF16)
    key, value = both[:, :HEAD_SIZE], both[:, HEAD_SIZE:]
    scale = HEAD_SIZE ** (-0.5)
    raw = mm(key, query_t)
    scores = jnp.concatenate(
        [
            raw[b * rows : (b + 1) * rows] * (scale * LOG2_E) + jnp.where(mask_ref[0, b] > 0, 0.0, -1e30)
            for b in range(blocks)
        ],
        axis=0,
    )
    highest = jnp.max(scores, axis=0, keepdims=True)
    raised = jnp.exp2(scores - highest)
    prob = raised * (1.0 / jnp.sum(raised, axis=0, keepdims=True))
    weights = prob.astype(BF16)
    attended_t = mm(value, weights, TN).astype(BF16)
    delta = jnp.sum(g_t.astype(F32) * attended_t.astype(F32), axis=0, keepdims=True)
    dscore = (prob * (mm(value, g_t) - delta) * scale).astype(BF16)
    dquery_t = mm(key, dscore, TN).astype(BF16)
    dquery = dquery_t.astype(F32).T.astype(BF16)
    dboth = jnp.concatenate([mm(dscore, query), mm(weights, g)], axis=1).astype(BF16)
    total[...] += mm(attended_t.astype(F32).T.astype(BF16), wo_ref[...])
    grads[...] += mm(dboth, w_both, NT)
    grads[:rows] += mm(dquery, wq_ref[...], NT)
    width = grad_out.shape[1]
    split = (-1, 2, chunk, HEAD_SIZE)
    dwq = mm(x_turned[:, :rows], dquery).reshape(split)
    dwb = mm(x_turned[...], dboth)
    dwk = dwb[:, :HEAD_SIZE].reshape(split)
    dwv = dwb[:, HEAD_SIZE:].reshape(split)
    dwo = mm(attended_t, grad_out).reshape(-1, 2, chunk, width)
    for c in range(2):
        for m, part in enumerate((dwq, dwk, dwv)):
            qkv_ref[c, m] = part[:, c].reshape(width // 2, HEAD_SIZE).astype(BF16)
        out_ref[c] = dwo[:, c].reshape(HEAD_SIZE // 2, width).astype(BF16)

    @pl.when(head == pl.num_programs(0) - 1)
    def _():
        updated_ref[...] = (state_ref[...].astype(F32) + total[...]).astype(BF16)
        own_grad_ref[...] = grads[:rows]
        near_grad_ref[...] = grads[rows:].reshape(near_grad_ref.shape).astype(BF16)


def attend(mask, tiles, state, grad_out, w_query, w_key, w_value, w_out, chunk):
    rows, width = state.shape
    near = len(tiles)
    whole = lambda: pl.BlockSpec((rows, width), lambda h: (0, 0))
    columns = lambda: pl.BlockSpec((width, HEAD_SIZE), lambda h: (0, h))
    return pl.pallas_call(
        functools.partial(attend_kernel, chunk),
        grid=(HEADS,),
        in_specs=[pl.BlockSpec(memory_space=pltpu.SMEM)]
        + [whole() for _ in range(near + 2)]
        + [columns(), columns(), columns(), pl.BlockSpec((HEAD_SIZE, width), lambda h: (h, 0))],
        out_specs=[
            whole(),
            whole(),
            pl.BlockSpec((near - 1, rows, width), lambda h: (0, 0, 0)),
            pl.BlockSpec((2, 3, width // 2, HEAD_SIZE), lambda h: (0, 0, 0, h)),
            pl.BlockSpec((2, HEAD_SIZE // 2, width), lambda h: (0, h, 0)),
        ],
        out_shape=(
            jax.ShapeDtypeStruct((rows, width), BF16),
            jax.ShapeDtypeStruct((rows, width), F32),
            jax.ShapeDtypeStruct((near - 1, rows, width), BF16),
            jax.ShapeDtypeStruct((2, 3, width // 2, width), BF16),
            jax.ShapeDtypeStruct((2, width // 2, width), BF16),
        ),
        scratch_shapes=[
            pltpu.VMEM((near * rows, width), BF16),
            pltpu.VMEM((width, near * rows), BF16),
            pltpu.VMEM((near * rows, width), F32),
            pltpu.VMEM((rows, width), F32),
        ],
        compiler_params=params(),
        name="attend",
    )(mask, *tiles, state, grad_out, w_query, w_key, w_value, w_out)


def finish_kernel(own_ref, up_ref, down_ref, left_ref, right_ref, normed_ref, inverse_ref, gain_ref, grad_ref, high_ref, low_ref, state_grad_ref, slot_ref):
    total = own_ref[...]
    for ref in (up_ref, down_ref, left_ref, right_ref):
        total = total + ref[...].astype(F32)
    grad = total * gain_ref[...].astype(F32)
    normed = normed_ref[...]
    grad = inverse_ref[:, :1] * (grad - normed * jnp.mean(grad * normed, axis=-1, keepdims=True))
    state_grad_ref[...] = (grad_ref[...].astype(F32) + grad).astype(BF16)
    top = grad.astype(BF16)
    rest = (grad - top.astype(F32)).astype(BF16)
    slot_ref[...] = (mm(high_ref[...], top, TN) + (mm(high_ref[...], rest, TN) + mm(low_ref[...], top, TN))).astype(BF16)


def finish(own, near, normed, inverse, gain, grad_out, high, low):
    rows, width = own.shape
    return pl.pallas_call(
        finish_kernel,
        out_shape=(
            jax.ShapeDtypeStruct((rows, width), BF16),
            jax.ShapeDtypeStruct((high.shape[1], width), BF16),
        ),
        compiler_params=params(),
        name="finish",
    )(own, *near, normed, inverse, gain, grad_out, high, low)


def exchange(chunks, axis):
    count = chunks.shape[0]
    here = lax.axis_index(axis)
    arrived = [
        lax.ppermute(
            lax.dynamic_index_in_dim(chunks, (here + step) % count, 0, keepdims=False),
            axis,
            [(i, (i + step) % count) for i in range(count)],
        )
        for step in range(1, count)
    ]
    total = lax.dynamic_index_in_dim(chunks, here, 0, keepdims=False).astype(F32)
    for piece in arrived:
        total = total + piece.astype(F32)
    return total


def passed_along(block, axis, distance):
    count = lax.axis_size(axis)
    route = [(i, i + distance) for i in range(count) if 0 <= i + distance < count]
    return lax.ppermute(block, axis, route)


TY = ("x_hi", "y")
TX = ("z", "x_lo", "core")
X = ("x_hi", "x_lo")


def reduce_weights(qkv, out):
    width = qkv.shape[-1]
    whole = jnp.concatenate([qkv, out[:, None]], axis=1)
    total = exchange(whole, "core").astype(BF16)
    sizes = [lax.axis_size(a) for a in ("x_hi", "y", "z", "x_lo")]
    chunk = total.shape[1] // (sizes[0] * sizes[1] * sizes[2] * sizes[3])
    total = total.reshape(4, *sizes, chunk, width)
    total = exchange(jnp.moveaxis(total, 3, 0), "z").astype(BF16)
    total = exchange(jnp.moveaxis(total, 2, 0), "y").astype(BF16)
    total = jnp.transpose(total, (1, 2, 0, 3, 4)).reshape(sizes[0] * sizes[3], 4, chunk, width)
    return exchange(total, X)


def body(
    region_state,
    global_latent,
    send_rows,
    recv_slots,
    regrid_weight,
    window_mask,
    norm_gain,
    w_query,
    w_key,
    w_value,
    w_out,
    out_grad,
):
    state, grad_out = region_state[0, 0], out_grad[0, 0]
    rows, width = state.shape
    gain = norm_gain[None]
    devices = lax.axis_size(TY + TX)
    outgoing = pick_rows(send_rows, global_latent)
    incoming = lax.all_to_all(outgoing, TY + TX, split_axis=0, concat_axis=0, tiled=True)
    normed_in, normed, inverse, high, low = blend_norm(
        recv_slots.reshape(rows, -1), regrid_weight[0, 0], incoming, state, gain
    )
    tiles = (
        normed_in,
        passed_along(normed_in, TY, 1),
        passed_along(normed_in, TY, -1),
        passed_along(normed_in, TX, 1),
        passed_along(normed_in, TX, -1),
    )
    updated, own, near, qkv, out = attend(
        window_mask[0], tiles, state, grad_out, w_query, w_key, w_value, w_out, width // devices
    )
    weight_grads = reduce_weights(qkv, out)
    returned = (
        passed_along(near[0], TY, -1),
        passed_along(near[1], TY, 1),
        passed_along(near[2], TX, -1),
        passed_along(near[3], TX, 1),
    )
    state_grad, slots = finish(own, returned, normed, inverse, gain, grad_out, high, low)
    sent_back = lax.all_to_all(slots, TY + TX, split_axis=0, concat_axis=0, tiled=True)
    global_grad = add_rows(send_rows, sent_back, global_latent.shape[0])
    return (updated[None, None], state_grad[None, None], global_grad, weight_grads)


def solution(mesh):
    ty, tx = mesh.devices.shape
    y, z = max(ty // 2, 1), tx // 4
    fine = jax.sharding.Mesh(mesh.devices.reshape(ty // y, y, z, 2, 2), TY + TX)
    tiles = P(TY, TX)
    flat = P(TY + TX)
    return jax.shard_map(
        body,
        mesh=fine,
        in_specs=(tiles, flat, flat, tiles, tiles, tiles, P(), P(), P(), P(), P(), tiles),
        out_specs=(tiles, tiles, flat, P(None, TY + TX)),
        check_vma=False,
    )
```

time: 1100 us -> 264 us (0.24)
  waiting for transfers between devices: 693 us -> 84.9 us
  matrix products: 103 us -> 0 us
  local copies, waits for them, and re-layouts: 105 us -> 14 us
  Pallas kernels: 0 us -> 66.1 us
  other arithmetic: 63.8 us -> 14.5 us
  starting transfers between devices: 111 us -> 80.8 us
  between operations: 15.1 us -> 0.96 us
    reduce_scatter x1 -> x0, waiting for transfers between devices: 581 us -> none  [body(): lax.psum_scatter(partial_grads, ('ty', 'tx'), scatter_dimension=1, tiled=...]
    dot_general x60 -> x0, matrix products: 103 us -> none  [the longest x8 18.6 us: one_head(): key_part = jnp.dot(dscore.T, query_h, preferred_element_type=jnp.float32)]
    pallas_call x0 -> x5, Pallas kernels: none -> 66.1 us  [the longest x1 46.2 us: attend(): pl.pallas_call(functools.partial(attend_kernel, chunk), grid=(HEADS,), in...]
    ppermute x4 -> x8, starting transfers between devices: 64.7 us -> 16.3 us  [passed_along(): return lax.ppermute(block, axis, route)]
    all_to_all x2, waiting for transfers between devices: 62.5 us -> 27.1 us  [the longest x1 27.1 us: body(): lax.all_to_all(outgoing, TY + TX, split_axis=0, concat_axis=0, tiled=True)]
    scatter-add x2 -> x0, other arithmetic: 23.9 us -> none  [the longest x1 12.8 us: body(): slot_grad = jnp.zeros((incoming.shape[0], model_width), jnp.float32).at[s...]
    ppermute x4 -> x10, waiting for transfers between devices: 25.1 us -> 46.4 us  [exchange(): lax.ppermute(lax.dynamic_index_in_dim(chunks, (here + step) % count, 0, k...]
    transpose x3 -> x1, local copies, waits for them, and re-layouts: 21 us -> 0.02 us  [reduce_weights(): jnp.transpose(total, (1, 2, 0, 3, 4))]
  transfers between devices with their start and end apart: 11 -> 20, of which waited for: 7 -> 7; matrix products, arithmetic and copies ran while one was open for 6% -> 6% of each run, Pallas kernels for 0% -> 4%
where the time goes in v1:
time: 264 us; the launch traced here: 261 us
  waiting for transfers between devices  84.9 us (32%)
  starting transfers between devices  80.8 us (31%)
  Pallas kernels  66.1 us (25%)
  other arithmetic  14.5 us (5%)
  local copies, waits for them, and re-layouts  14 us (5%)
    ppermute x10, waiting for transfers between devices, exchange(): lax.ppermute(lax.dynamic_index_in_dim(chunks, (here + step) % count, 0, k...  46.4 us
    pallas_call x1, Pallas kernels, attend(): pl.pallas_call(functools.partial(attend_kernel, chunk), grid=(HEADS,), in...  46.2 us
    all_to_all x1, starting transfers between devices, body(): lax.all_to_all(slots, TY + TX, split_axis=0, concat_axis=0, tiled=True)  28.4 us
    all_to_all x1, waiting for transfers between devices, body(): lax.all_to_all(outgoing, TY + TX, split_axis=0, concat_axis=0, tiled=True)  27.1 us
    ppermute x10, starting transfers between devices, exchange(): lax.ppermute(lax.dynamic_index_in_dim(chunks, (here + step) % count, 0, k...  25 us
    ppermute x8, starting transfers between devices, passed_along(): return lax.ppermute(block, axis, route)  16.3 us
    ppermute x8, waiting for transfers between devices, passed_along(): return lax.ppermute(block, axis, route)  11.4 us
    all_to_all x1, starting transfers between devices, body(): lax.all_to_all(outgoing, TY + TX, split_axis=0, concat_axis=0, tiled=True)  11.1 us
  transfers between devices with their start and end apart: 20, of which 7 were waited for; matrix products, arithmetic and copies ran while one was open for 6% of the time, Pallas kernels for 4%

profile of v1, /device:TPU:0, one launch (start us, length us, event | category | flops | bytes accessed | tf_op | source)
XLA Modules:
  0.0 261.2 jit_solution(16273575269607115983)
XLA Ops:
  0.7 4.5 %pick_rows.1 = bf16[1024,1024]{1,0:T(8,128)(2,1)} custom-call(s32[1,1024]{1,0:T(1,128)} %rows_ref.3, bf16[512,1024]{1,0:T(8,128)(2,1)} %table_ref.1), custom_call_target="tpu_custom_call" | custom-call | tf_op jit(solution)/shard_map/pick_rows/pallas_call | solution.py:36
  5.1 11.1 %all-to-all-start = ((bf16[128,8,1024]{2,1,0:T(8,128)(2,1)}), bf16[128,8,1024]{2,1,0:T(8,128)(2,1)S(1)}, u32[]{:S(2)}, u32[]{:S(2)}) async-start(bf16[128,8,1024]{2,1,0:T(8,128)(2,1)} %bitcast.65), calls=%async_computation | async-start | bytes 4194304 | tf_op jit(solution)/shard_map/all_to_all | solution.py:297
  19.6 27.1 %all-to-all-done = bf16[128,8,1024]{2,1,0:T(8,128)(2,1)S(1)} async-done(((bf16[128,8,1024]{2,1,0:T(8,128)(2,1)}), bf16[128,8,1024]{2,1,0:T(8,128)(2,1)S(1)}, u32[]{:S(2)}, u32[]{:S(2)}) %all-to-all-start) | async-done | bytes 2097184 | tf_op jit(solution)/shard_map/all_to_all | solution.py:297
  48.1 5.0 %blend_norm.1 = (bf16[256,1024]{1,0:T(8,128)(2,1)}, f32[256,1024]{1,0:T(8,128)}, f32[256,128]{1,0:T(8,128)}, bf16[256,1024]{1,0:T(8,128)(2,1)}, bf16[256,1024]{1,0:T(8,128)(2,1)}) custom-call(s32[256,4]{1,0:T(8,128)} %reshape.45.slots_ref, f32[256,4]{1,0:T(8,128)} %bitcast.73, bf16[1024,1024]{1,0:T(8,128)(2,1)} %bitcast.64, bf16[256,1024]{1,0:T(8,128)(2,1)} %bitcast.69, ...), custom_call_target="tpu_custom_call" | custom-call | tf_op jit(solution)/shard_map/blend_norm/pallas_call | solution.py:95
  58.4 7.3 %collective-permute-done.up_ref = bf16[256,1024]{1,0:T(8,128)(2,1)S(1)} collective-permute-done((bf16[256,1024]{1,0:T(8,128)(2,1)}, bf16[256,1024]{1,0:T(8,128)(2,1)S(1)}, u32[]{:S(2)}, u32[]{:S(2)}) %collective-permute-start) | collective-permute-done | bytes 524320 | tf_op jit(solution)/shard_map/ppermute | solution.py:257
  65.7 4.0 %collective-permute-done.1.down_ref = bf16[256,1024]{1,0:T(8,128)(2,1)S(1)} collective-permute-done((bf16[256,1024]{1,0:T(8,128)(2,1)}, bf16[256,1024]{1,0:T(8,128)(2,1)S(1)}, u32[]{:S(2)}, u32[]{:S(2)}) %collective-permute-start.1) | collective-permute-done | bytes 524320 | tf_op jit(solution)/shard_map/ppermute | solution.py:257
  71.0 46.2 %attend.1 = (bf16[256,1024]{1,0:T(8,128)(2,1)}, f32[256,1024]{1,0:T(8,128)}, bf16[4,256,1024]{2,1,0:T(8,128)(2,1)}, bf16[2,3,512,1024]{3,2,1,0:T(8,128)(2,1)}, bf16[2,512,1024]{2,1,0:T(8,128)(2,1)}) custom-call(s32[1,5]{1,0:T(1,128)} %bitcast.74, bf16[256,1024]{1,0:T(8,128)(2,1)} %get-tuple-element.16.own_ref, bf16[256,1024]{1,0:T(8,128)(2,1)} %copy-done.6, ...), custom_call_target="tpu_custom_call" | custom-call | tf_op jit(solution)/shard_map/attend/pallas_call | solution.py:180
  117.3 4.6 %fusion.2 = bf16[4,512,1024]{2,1,0:T(8,128)(2,1)} fusion(s32[]{:T(128)S(6)} %select_n.91, bf16[2,3,512,1024]{3,2,1,0:T(8,128)(2,1)} %get-tuple-element.26, bf16[2,1,512,1024]{3,2,1,0:T(8,128)(2,1)} %bitcast.61), kind=kLoop, calls=%fused_computation.7 | loop fusion | flops 2097152 | bytes 12582916 | tf_op jit(solution)/shard_map/jit(dynamic_index_in_dim)/squeeze | solution.py:242
  123.0 1.7 slice_bitcast_fusion
  125.9 5.2 %collective-permute-start.5 = (bf16[256,1024]{1,0:T(8,128)(2,1)S(1)}, bf16[256,1024]{1,0:T(8,128)(2,1)S(1)}, u32[]{:S(2)}, u32[]{:S(2)}) collective-permute-start(bf16[256,1024]{1,0:T(8,128)(2,1)S(1)} %get-tuple-element.33), channel_id=1, source_target_pairs={{0,16},{16,32},{32,48},{48,64},{64,80},{80,96},{96,112},{1,17},{17... | collective-permute-start | bytes 1572872 | tf_op jit(solution)/shard_map/ppermute | solution.py:257
  132.5 3.2 %collective-permute-start.7 = (bf16[256,1024]{1,0:T(8,128)(2,1)S(1)}, bf16[256,1024]{1,0:T(8,128)(2,1)S(1)}, u32[]{:S(2)}, u32[]{:S(2)}) collective-permute-start(bf16[256,1024]{1,0:T(8,128)(2,1)S(1)} %get-tuple-element.31), channel_id=1, source_target_pairs={{0,1},{1,2},{2,3},{3,4},{4,5},{5,6},{6,7},{7,8},{8,9},{9,10},{10,1... | collective-permute-start | bytes 1572872 | tf_op jit(solution)/shard_map/ppermute | solution.py:257
  135.7 4.2 %fusion = bf16[4,512,1024]{2,1,0:T(8,128)(2,1)S(1)} fusion(bf16[4,512,1024]{2,1,0:T(8,128)(2,1)} %collective-permute-done.8, s32[]{:T(128)S(6)} %select_n.89, bf16[2,3,512,1024]{3,2,1,0:T(8,128)(2,1)} %get-tuple-element.26, bf16[2,1,512,1024]{3,2,1,0:T(8,128)(2,1)S(1)} %bitcast.62), kind=kLoop, calls=%fused_computation.5 | loop fusion | flops 10485760 | bytes 16777220 | tf_op jit(solution)/shard_map/convert_element_type | solution.py:268
  139.9 2.0 copy-done
  141.9 1.8 dynamic-slice_bitcast_fusion.2
  143.7 2.0 collective-permute-start.11
  148.3 6.5 %finish.1 = (bf16[256,1024]{1,0:T(8,128)(2,1)}, bf16[1024,1024]{1,0:T(8,128)(2,1)}) custom-call(f32[256,1024]{1,0:T(8,128)} %get-tuple-element.18.own_ref, bf16[256,1024]{1,0:T(8,128)(2,1)} %copy-done.4, bf16[256,1024]{1,0:T(8,128)(2,1)} %copy-done.5, bf16[256,1024]{1,0:T(8,128)(2,1)} %copy-done.7, bf16[256,1024]{1,0:T(8,128)(2,1)} %copy-done.10, ...), custom_call_target="tpu_custom_call" | custom-call | tf_op jit(solution)/shard_map/finish/pallas_call | solution.py:226
  154.8 28.4 %all-to-all-start.1 = ((bf16[128,8,1024]{2,1,0:T(8,128)(2,1)}), bf16[128,8,1024]{2,1,0:T(8,128)(2,1)S(1)}, u32[]{:S(2)}, u32[]{:S(2)}) async-start(bf16[128,8,1024]{2,1,0:T(8,128)(2,1)} %bitcast.68), calls=%async_computation.1 | async-start | bytes 4194304 | tf_op jit(solution)/shard_map/all_to_all | solution.py:319
  183.3 32.4 %collective-permute-done.9 = bf16[4,2,4,2,8,1024]{5,4,3,2,1,0:T(8,128)(2,1)} collective-permute-done((bf16[4,2,4,2,8,1024]{5,4,3,2,1,0:T(8,128)(2,1)S(1)}, bf16[4,2,4,2,8,1024]{5,4,3,2,1,0:T(8,128)(2,1)}, u32[]{:S(2)}, u32[]{:S(2)}) %collective-permute-start.9) | collective-permute-done | bytes 1048608 | tf_op jit(solution)/shard_map/ppermute | solution.py:241
  215.8 3.1 %fusion.7 = bf16[4,2,4,2,8,1024]{5,4,3,2,1,0:T(8,128)(2,1)S(1)} fusion(bf16[4,2,4,2,8,1024]{5,4,3,2,1,0:T(8,128)(2,1)} %collective-permute-done.11, bf16[4,2,4,2,8,1024]{5,4,3,2,1,0:T(8,128)(2,1)} %collective-permute-done.10, bf16[4,2,4,2,8,1024]{5,4,3,2,1,0:T(8,128)(2,1)} %collective-permute-done.9, bf16[4,2,4,4,2,8,1024]{6,5,4,3,2,1,0:T(8,128)(2,1)} %bitcast.60, ...), kind=kLoop, calls=%fused_computation.13 | loop fusion | flops 4194304 | bytes 5242884 | tf_op jit(solution)/shard_map/convert_element_type | solution.py:272
  219.7 17.2 %collective-permute-start.14 = (bf16[4,2,2,8,1024]{4,3,2,1,0:T(8,128)(2,1)}, bf16[4,2,2,8,1024]{4,3,2,1,0:T(8,128)(2,1)}, u32[]{:S(2)}, u32[]{:S(2)}) collective-permute-start(bf16[4,2,2,8,1024]{4,3,2,1,0:T(8,128)(2,1)} %get-tuple-element.36), channel_id=1, source_target_pairs={{0,48},{16,0},{32,16},{48,32},{1,49},{17,1},{33,17},{49,33},{2,50}... | collective-permute-start | bytes 786440 | tf_op jit(solution)/shard_map/ppermute | solution.py:241
  237.8 10.5 %collective-permute-done.14 = bf16[4,2,2,8,1024]{4,3,2,1,0:T(8,128)(2,1)} collective-permute-done((bf16[4,2,2,8,1024]{4,3,2,1,0:T(8,128)(2,1)}, bf16[4,2,2,8,1024]{4,3,2,1,0:T(8,128)(2,1)}, u32[]{:S(2)}, u32[]{:S(2)}) %collective-permute-start.14) | collective-permute-done | bytes 262176 | tf_op jit(solution)/shard_map/ppermute | solution.py:241
  248.3 3.2 %collective-permute-done.12 = bf16[4,2,2,8,1024]{4,3,2,1,0:T(8,128)(2,1)} collective-permute-done((bf16[4,2,2,8,1024]{4,3,2,1,0:T(8,128)(2,1)S(1)}, bf16[4,2,2,8,1024]{4,3,2,1,0:T(8,128)(2,1)}, u32[]{:S(2)}, u32[]{:S(2)}) %collective-permute-start.12) | collective-permute-done | bytes 262176 | tf_op jit(solution)/shard_map/ppermute | solution.py:241
  252.9 2.1 collective-permute-start.16
  256.4 3.8 %add_rows.1 = bf16[512,1024]{1,0:T(8,128)(2,1)} custom-call(s32[1,1024]{1,0:T(1,128)} %rows_ref.3, bf16[1024,1024]{1,0:T(8,128)(2,1)} %bitcast.63), custom_call_target="tpu_custom_call" | custom-call | tf_op jit(solution)/shard_map/add_rows/pallas_call | solution.py:59
  (66 shorter events, 22.9 us)
Async XLA Ops:
  0.6 16.2 %copy-start.13 = (s32[1,1,1024]{2,1,0:T(1,128)S(1)}, s32[1,1,1024]{2,1,0:T(1,128)}, u32[]{:S(2)}) copy-start(s32[1,1,1024]{2,1,0:T(1,128)} %param.15) | copy-start | bytes 12292
  0.6 17.6 %copy-start.12 = (f32[1,1,256,4]{2,3,1,0:T(4,128)S(1)}, f32[1,1,256,4]{2,3,1,0:T(4,128)}, u32[]{:S(2)}) copy-start(f32[1,1,256,4]{2,3,1,0:T(4,128)} %param.16) | copy-start | bytes 12292
  0.7 18.4 %copy-start.14 = (bf16[1024]{0:T(1024)(128)(2,1)S(1)}, bf16[1024]{0:T(1024)(128)(2,1)}, u32[]{:S(2)}) copy-start(bf16[1024]{0:T(1024)(128)(2,1)} %param.18) | copy-start | bytes 6148
  5.1 41.6 %all-to-all-start = ((bf16[128,8,1024]{2,1,0:T(8,128)(2,1)}), bf16[128,8,1024]{2,1,0:T(8,128)(2,1)S(1)}, u32[]{:S(2)}, u32[]{:S(2)}) async-start(bf16[128,8,1024]{2,1,0:T(8,128)(2,1)} %bitcast.65), calls=%async_computation | async-start | bytes 4194304 | tf_op jit(solution)/shard_map/all_to_all | solution.py:297
  53.1 12.6 %collective-permute-start = (bf16[256,1024]{1,0:T(8,128)(2,1)}, bf16[256,1024]{1,0:T(8,128)(2,1)S(1)}, u32[]{:S(2)}, u32[]{:S(2)}) collective-permute-start(bf16[256,1024]{1,0:T(8,128)(2,1)} %get-tuple-element.16.own_ref), channel_id=1, source_target_pairs={{0,16},{16,32},{32,48},{48,64},{64,80},{80,96},{96,112},{1,17},{17... | collective-permute-start | bytes 1572872 | tf_op jit(solution)/shard_map/ppermute | solution.py:257
  54.4 15.3 %collective-permute-start.1 = (bf16[256,1024]{1,0:T(8,128)(2,1)}, bf16[256,1024]{1,0:T(8,128)(2,1)S(1)}, u32[]{:S(2)}, u32[]{:S(2)}) collective-permute-start(bf16[256,1024]{1,0:T(8,128)(2,1)} %get-tuple-element.16.own_ref), channel_id=1, source_target_pairs={{16,0},{32,16},{48,32},{64,48},{80,64},{96,80},{112,96},{17,1},{33... | collective-permute-start | bytes 1572872 | tf_op jit(solution)/shard_map/ppermute | solution.py:257
  55.7 14.1 %collective-permute-start.2 = (bf16[256,1024]{1,0:T(8,128)(2,1)}, bf16[256,1024]{1,0:T(8,128)(2,1)S(1)}, u32[]{:S(2)}, u32[]{:S(2)}) collective-permute-start(bf16[256,1024]{1,0:T(8,128)(2,1)} %get-tuple-element.16.own_ref), channel_id=1, source_target_pairs={{0,1},{1,2},{2,3},{3,4},{4,5},{5,6},{6,7},{7,8},{8,9},{9,10},{10,1... | collective-permute-start | bytes 1572872 | tf_op jit(solution)/shard_map/ppermute | solution.py:257
  57.1 12.7 %collective-permute-start.3 = (bf16[256,1024]{1,0:T(8,128)(2,1)}, bf16[256,1024]{1,0:T(8,128)(2,1)S(1)}, u32[]{:S(2)}, u32[]{:S(2)}) collective-permute-start(bf16[256,1024]{1,0:T(8,128)(2,1)} %get-tuple-element.16.own_ref), channel_id=1, source_target_pairs={{1,0},{2,1},{3,2},{4,3},{5,4},{6,5},{7,6},{8,7},{9,8},{10,9},{11,1... | collective-permute-start | bytes 1572872 | tf_op jit(solution)/shard_map/ppermute | solution.py:257
  121.9 13.9 %copy-start.1 = (bf16[2,512,1024]{2,1,0:T(8,128)(2,1)S(1)}, bf16[2,512,1024]{2,1,0:T(8,128)(2,1)}, u32[]{:S(2)}) copy-start(bf16[2,512,1024]{2,1,0:T(8,128)(2,1)} %get-tuple-element.27) | copy-start | bytes 6291460
  121.9 13.9 %collective-permute-start.8 = (bf16[4,512,1024]{2,1,0:T(8,128)(2,1)}, bf16[4,512,1024]{2,1,0:T(8,128)(2,1)}, u32[]{:S(2)}, u32[]{:S(2)}) collective-permute-start(bf16[4,512,1024]{2,1,0:T(8,128)(2,1)} %fusion.2), channel_id=1, source_target_pairs={{0,1},{1,0},{2,3},{3,2},{4,5},{5,4},{6,7},{7,6},{8,9},{9,8},{10,11... | collective-permute-start | bytes 12582920 | tf_op jit(solution)/shard_map/ppermute | solution.py:241
  124.6 21.1 %collective-permute-start.4 = (bf16[256,1024]{1,0:T(8,128)(2,1)S(1)}, bf16[256,1024]{1,0:T(8,128)(2,1)S(1)}, u32[]{:S(2)}, u32[]{:S(2)}) collective-permute-start(bf16[256,1024]{1,0:T(8,128)(2,1)S(1)} %get-tuple-element.34), channel_id=1, source_target_pairs={{16,0},{32,16},{48,32},{64,48},{80,64},{96,80},{112,96},{17,1},{33... | collective-permute-start | bytes 1572872 | tf_op jit(solution)/shard_map/ppermute | solution.py:257
  125.9 21.2 %collective-permute-start.5 = (bf16[256,1024]{1,0:T(8,128)(2,1)S(1)}, bf16[256,1024]{1,0:T(8,128)(2,1)S(1)}, u32[]{:S(2)}, u32[]{:S(2)}) collective-permute-start(bf16[256,1024]{1,0:T(8,128)(2,1)S(1)} %get-tuple-element.33), channel_id=1, source_target_pairs={{0,16},{16,32},{32,48},{48,64},{64,80},{80,96},{96,112},{1,17},{17... | collective-permute-start | bytes 1572872 | tf_op jit(solution)/shard_map/ppermute | solution.py:257
  131.2 16.2 %collective-permute-start.6 = (bf16[256,1024]{1,0:T(8,128)(2,1)S(1)}, bf16[256,1024]{1,0:T(8,128)(2,1)S(1)}, u32[]{:S(2)}, u32[]{:S(2)}) collective-permute-start(bf16[256,1024]{1,0:T(8,128)(2,1)S(1)} %get-tuple-element.32), channel_id=1, source_target_pairs={{1,0},{2,1},{3,2},{4,3},{5,4},{6,5},{7,6},{8,7},{9,8},{10,9},{11,1... | collective-permute-start | bytes 1572872 | tf_op jit(solution)/shard_map/ppermute | solution.py:257
  132.5 14.9 %collective-permute-start.7 = (bf16[256,1024]{1,0:T(8,128)(2,1)S(1)}, bf16[256,1024]{1,0:T(8,128)(2,1)S(1)}, u32[]{:S(2)}, u32[]{:S(2)}) collective-permute-start(bf16[256,1024]{1,0:T(8,128)(2,1)S(1)} %get-tuple-element.31), channel_id=1, source_target_pairs={{0,1},{1,2},{2,3},{3,4},{4,5},{5,6},{6,7},{7,8},{8,9},{9,10},{10,1... | collective-permute-start | bytes 1572872 | tf_op jit(solution)/shard_map/ppermute | solution.py:257
  143.7 39.6 %collective-permute-start.11 = (bf16[4,2,4,2,8,1024]{5,4,3,2,1,0:T(8,128)(2,1)}, bf16[4,2,4,2,8,1024]{5,4,3,2,1,0:T(8,128)(2,1)}, u32[]{:S(2)}, u32[]{:S(2)}) collective-permute-start(bf16[4,2,4,2,8,1024]{5,4,3,2,1,0:T(8,128)(2,1)} %get-tuple-element.29), channel_id=1, source_target_pairs={{0,12},{4,0},{8,4},{12,8},{1,13},{5,1},{9,5},{13,9},{2,14},{6,2},{... | collective-permute-start | bytes 3145736 | tf_op jit(solution)/shard_map/ppermute | solution.py:241
  145.7 37.6 %collective-permute-start.10 = (bf16[4,2,4,2,8,1024]{5,4,3,2,1,0:T(8,128)(2,1)}, bf16[4,2,4,2,8,1024]{5,4,3,2,1,0:T(8,128)(2,1)}, u32[]{:S(2)}, u32[]{:S(2)}) collective-permute-start(bf16[4,2,4,2,8,1024]{5,4,3,2,1,0:T(8,128)(2,1)} %get-tuple-element.30), channel_id=1, source_target_pairs={{0,8},{4,12},{8,0},{12,4},{1,9},{5,13},{9,1},{13,5},{2,10},{6,14},... | collective-permute-start | bytes 3145736 | tf_op jit(solution)/shard_map/ppermute | solution.py:241
  147.2 68.6 %collective-permute-start.9 = (bf16[4,2,4,2,8,1024]{5,4,3,2,1,0:T(8,128)(2,1)S(1)}, bf16[4,2,4,2,8,1024]{5,4,3,2,1,0:T(8,128)(2,1)}, u32[]{:S(2)}, u32[]{:S(2)}) collective-permute-start(bf16[4,2,4,2,8,1024]{5,4,3,2,1,0:T(8,128)(2,1)S(1)} %get-tuple-element.28), channel_id=1, source_target_pairs={{0,4},{4,8},{8,12},{12,0},{1,5},{5,9},{9,13},{13,1},{2,6},{6,10},{... | collective-permute-start | bytes 3145736 | tf_op jit(solution)/shard_map/ppermute | solution.py:241
  154.8 100.2 %all-to-all-start.1 = ((bf16[128,8,1024]{2,1,0:T(8,128)(2,1)}), bf16[128,8,1024]{2,1,0:T(8,128)(2,1)S(1)}, u32[]{:S(2)}, u32[]{:S(2)}) async-start(bf16[128,8,1024]{2,1,0:T(8,128)(2,1)} %bitcast.68), calls=%async_computation.1 | async-start | bytes 4194304 | tf_op jit(solution)/shard_map/all_to_all | solution.py:319
  219.7 28.6 %collective-permute-start.14 = (bf16[4,2,2,8,1024]{4,3,2,1,0:T(8,128)(2,1)}, bf16[4,2,2,8,1024]{4,3,2,1,0:T(8,128)(2,1)}, u32[]{:S(2)}, u32[]{:S(2)}) collective-permute-start(bf16[4,2,2,8,1024]{4,3,2,1,0:T(8,128)(2,1)} %get-tuple-element.36), channel_id=1, source_target_pairs={{0,48},{16,0},{32,16},{48,32},{1,49},{17,1},{33,17},{49,33},{2,50}... | collective-permute-start | bytes 786440 | tf_op jit(solution)/shard_map/ppermute | solution.py:241
  237.0 11.3 %collective-permute-start.13 = (bf16[4,2,2,8,1024]{4,3,2,1,0:T(8,128)(2,1)}, bf16[4,2,2,8,1024]{4,3,2,1,0:T(8,128)(2,1)}, u32[]{:S(2)}, u32[]{:S(2)}) collective-permute-start(bf16[4,2,2,8,1024]{4,3,2,1,0:T(8,128)(2,1)} %get-tuple-element.37), channel_id=1, source_target_pairs={{0,32},{16,48},{32,0},{48,16},{1,33},{17,49},{33,1},{49,17},{2,34}... | collective-permute-start | bytes 786440 | tf_op jit(solution)/shard_map/ppermute | solution.py:241
  237.0 14.5 %collective-permute-start.12 = (bf16[4,2,2,8,1024]{4,3,2,1,0:T(8,128)(2,1)S(1)}, bf16[4,2,2,8,1024]{4,3,2,1,0:T(8,128)(2,1)}, u32[]{:S(2)}, u32[]{:S(2)}) collective-permute-start(bf16[4,2,2,8,1024]{4,3,2,1,0:T(8,128)(2,1)S(1)} %get-tuple-element.35), channel_id=1, source_target_pairs={{0,16},{16,32},{32,48},{48,0},{1,17},{17,33},{33,49},{49,1},{2,18}... | collective-permute-start | bytes 786440 | tf_op jit(solution)/shard_map/ppermute | solution.py:241
  252.9 7.4 %collective-permute-start.17 = (bf16[4,8,1024]{2,1,0:T(8,128)(2,1)S(1)}, bf16[4,8,1024]{2,1,0:T(8,128)(2,1)S(1)}, u32[]{:S(2)}, u32[]{:S(2)}) collective-permute-start(bf16[4,8,1024]{2,1,0:T(8,128)(2,1)S(1)} %get-tuple-element.39), channel_id=1, source_target_pairs={{0,66},{2,0},{64,2},{66,64},{1,67},{3,1},{65,3},{67,65},{4,70},{6,... | collective-permute-start | bytes 196616 | tf_op jit(solution)/shard_map/ppermute | solution.py:241
  252.9 7.3 %collective-permute-start.16 = (bf16[4,8,1024]{2,1,0:T(8,128)(2,1)S(1)}, bf16[4,8,1024]{2,1,0:T(8,128)(2,1)S(1)}, u32[]{:S(2)}, u32[]{:S(2)}) collective-permute-start(bf16[4,8,1024]{2,1,0:T(8,128)(2,1)S(1)} %get-tuple-element.40), channel_id=1, source_target_pairs={{0,64},{2,66},{64,0},{66,2},{1,65},{3,67},{65,1},{67,3},{4,68},{6,... | collective-permute-start | bytes 196616 | tf_op jit(solution)/shard_map/ppermute | solution.py:241
  255.0 5.5 %collective-permute-start.15 = (bf16[4,8,1024]{2,1,0:T(8,128)(2,1)S(1)}, bf16[4,8,1024]{2,1,0:T(8,128)(2,1)S(1)}, u32[]{:S(2)}, u32[]{:S(2)}) collective-permute-start(bf16[4,8,1024]{2,1,0:T(8,128)(2,1)S(1)} %get-tuple-element.38), channel_id=1, source_target_pairs={{0,2},{2,64},{64,66},{66,0},{1,3},{3,65},{65,67},{67,1},{4,6},{6,6... | collective-permute-start | bytes 196616 | tf_op jit(solution)/shard_map/ppermute | solution.py:241
  (11 other events, 16.1 us)
